TPU v7x, 256 devices: a whole 4x4x8 slice. The times are simulated.
256 devices in a mesh: section: 8 (over y, z_hi), vocab: 32 (over x, z_lo, core).
Axes of the slice: x: 4, y: 4, z: 8 (z_hi: 2, z_lo: 4; z = z_hi * 4 + z_lo), core: 2. Of those that a mesh axis runs over, the one named last changes fastest.
Arguments:
- hidden: bfloat16 [256, 4608], P('vocab', 'section'), may hold values from -6 to 6
- table: bfloat16 [256000, 4608], P(('vocab', 'section')), may hold values from -0.25 to 0.25
- token_ids: int32 [256], P('vocab'), may hold values from 0 to 255999
- targets: int32 [256], P('vocab'), may hold values from 0 to 255999
- input_grad: bfloat16 [256, 4608], P('vocab', 'section'), may hold values from -0.119628906 to 0.119628906
- projection: bfloat16 [4608, 256], replicated, may hold values from -0.09375 to 0.09375
Outputs:
- token_loss: float32 [256], P('vocab')
- hidden_grad: bfloat16 [256, 4608], P('vocab', 'section')
- low_rank: float32 [256000, 256], P(('vocab', 'section'))
All inputs are finite; a program needn't handle non-finite values.
Results may differ from a plain program's by a relative error of at most 0.0065.
Values may be sent and summed in bfloat16 or wider, within the bound.
A program may use at most 128 MiB of HBM per device.

v0:
```python
import math

import jax
import jax.numpy as jnp
from jax import lax
from jax.sharding import PartitionSpec as P


def per_device(hidden, table, token_ids, targets, input_grad, projection):
    rows_here = hidden.shape[0]
    width = projection.shape[0]
    slab = table.shape[0]
    hidden_cols, input_cols = (
        lax.all_gather(hidden, "section", axis=1, tiled=True),
        lax.all_gather(input_grad, "section", axis=1, tiled=True),
    )
    hidden_all, input_all, ids_all, targets_all = (
        lax.all_gather(hidden_cols, "vocab", axis=0, tiled=True),
        lax.all_gather(input_cols, "vocab", axis=0, tiled=True),
        lax.all_gather(token_ids, "vocab", axis=0, tiled=True),
        lax.all_gather(targets, "vocab", axis=0, tiled=True),
    )
    offset = (lax.axis_index("vocab") * lax.axis_size("section") + lax.axis_index("section")) * slab
    columns = offset + jnp.arange(slab, dtype=jnp.int32)
    raw = lax.dot_general(
        hidden_all, table, (((1,), (1,)), ((), ())), preferred_element_type=jnp.float32
    )
    capped = 30.0 * jnp.tanh(raw / 30.0)
    expo = jnp.exp(capped)
    target_hit = targets_all[:, None] == columns[None, :]
    local_total = jnp.sum(expo, axis=1)
    local_pick = jnp.sum(jnp.where(target_hit, capped, 0.0), axis=1)
    total, picked = lax.psum((local_total, local_pick), ("vocab", "section"))
    every_loss = jnp.log(total) - picked
    token_loss = lax.dynamic_slice_in_dim(
        every_loss, lax.axis_index("vocab") * rows_here, rows_here, 0
    )
    dlogit = (
        (expo / total[:, None] - target_hit.astype(jnp.float32)) * (1.0 - (capped / 30.0) ** 2)
    ).astype(jnp.bfloat16)
    summed_rows = lax.psum_scatter(
        jnp.dot(dlogit, table, preferred_element_type=jnp.float32),
        "vocab",
        scatter_dimension=0,
        tiled=True,
    )
    hidden_sum = lax.psum_scatter(summed_rows, "section", scatter_dimension=1, tiled=True)
    hidden_grad = hidden_sum.astype(jnp.bfloat16)
    id_hit = ids_all[:, None] == columns[None, :]
    head_grad = lax.dot_general(
        dlogit, hidden_all, (((0,), (0,)), ((), ())), preferred_element_type=jnp.float32
    )
    embed_grad = lax.dot_general(
        id_hit.astype(jnp.bfloat16),
        input_all,
        (((0,), (0,)), ((), ())),
        preferred_element_type=jnp.float32,
    )
    full_grad = head_grad + math.sqrt(width) * embed_grad
    upper_part = full_grad.astype(jnp.bfloat16)
    lower_part = (full_grad - upper_part.astype(jnp.float32)).astype(jnp.bfloat16)
    low_rank = jnp.dot(upper_part, projection, preferred_element_type=jnp.float32) + jnp.dot(
        lower_part, projection, preferred_element_type=jnp.float32
    )
    return (token_loss, hidden_grad, low_rank)


def solution(mesh):
    placed = (
        P("vocab", "section"),
        P(("vocab", "section"), None),
        P("vocab"),
        P("vocab"),
        P("vocab", "section"),
        P(),
    )
    return jax.shard_map(
        per_device,
        mesh=mesh,
        in_specs=placed,
        out_specs=(P("vocab"), P("vocab", "section"), P(("vocab", "section"), None)),
        check_vma=False,
    )
```

profile of v0, /device:TPU:1, one launch (start us, length us, event | category | flops | bytes accessed | tf_op | source)
XLA Modules:
  0.0 466.8 jit_solution(13816230962514931206)
XLA Ops:
  7.2 0.0 copy-start
  7.2 0.0 all-gather.5.cloned.1.call-start
  7.2 40.9 %all-gather = bf16[8,576,8]{1,2,0:T(8,128)(2,1)S(1)} all-gather(bf16[1,576,8]{1,2,0:T(8,128)(2,1)} %bitcast.26), channel_id=1, replica_groups=mesh['section'=8,'vocab'=32] {'section'}, dimensions={0}, use_global_device_ids=true | all-gather | bytes 82944 | tf_op jit(solution)/shard_map/all_gather | solution.py:14
  48.1 0.7 reshape.20
  48.9 0.0 all-gather.5.cloned.1.call-update
  48.9 0.0 all-gather.7.cloned.1.call-start
  49.0 38.3 %all-gather.1 = bf16[8,576,8]{1,2,0:T(8,128)(2,1)S(1)} all-gather(bf16[1,576,8]{1,2,0:T(8,128)(2,1)} %bitcast.27), channel_id=1, replica_groups=mesh['section'=8,'vocab'=32] {'section'}, dimensions={0}, use_global_device_ids=true | all-gather | bytes 82944 | tf_op jit(solution)/shard_map/all_gather | solution.py:15
  87.2 0.7 reshape.22
  88.0 0.0 all-gather.7.cloned.1.call-update
  88.0 0.0 reduce-scatter.5.cloned.1.call-start
  88.0 1.3 dynamic-slice
  90.0 0.9 dynamic-update-slice
  90.8 0.8 dynamic-update-slice.1
  91.7 25.0 %all-reduce.2 = (s32[256]{0:T(256)S(1)}, s32[256]{0:T(256)S(1)}) all-reduce(s32[256]{0:T(256)S(1)} %dynamic-update-slice, s32[256]{0:T(256)S(1)} %dynamic-update-slice.1), channel_id=1, replica_groups=mesh['section'=8,'vocab'=32] {'vocab'}, use_global_device_ids=true, to_apply=%add | all-reduce | flops 512 | bytes 4096
  116.7 0.6 all-gather.5.cloned.1.call-done
  117.3 6.2 %exponential_reduce_fusion = (f32[256]{0:T(256)S(1)}, f32[256]{0:T(256)S(1)}, f32[256,1000]{0,1:T(8,128)S(1)}) fusion(s32[1000]{0:T(1024)S(1)} %iota_add_fusion, s32[256]{0:T(256)S(1)} %get-tuple-element.5, bf16[256,4608]{1,0:T(8,128)(2,1)} %all-gather.5.cloned.1.call-done, bf16[1000,4608]{1,0:T(8,128)(2,1)} %param.7), kind=kOutput, calls=%fused_computation.16 | convolution fusion | flops 2360831488 | bytes 12606368 | tf_op jit(solution)/shard_map/dot_general | solution.py:25
  123.5 78.1 %all-reduce.3 = (f32[256]{0:T(256)S(1)}, f32[256]{0:T(256)S(1)}) all-reduce(f32[256]{0:T(256)S(1)} %get-tuple-element.4, f32[256]{0:T(256)S(1)} %get-tuple-element.3), channel_id=1, replica_groups=mesh['section'=8,'vocab'=32] {'vocab','section'}, use_global_device_ids=true, to_apply=%region_3.4 | all-reduce | flops 512 | bytes 4096 | tf_op jit(solution)/shard_map/psum | solution.py:33
  201.6 8.6 %fusion.17 = f32[256,4608]{1,0:T(8,128)} fusion(bf16[1000,4608]{1,0:T(8,128)(2,1)} %param.7, f32[256,1000]{0,1:T(8,128)S(1)} %get-tuple-element.9, f32[256]{0:T(256)S(1)} %get-tuple-element.8, s32[256]{0:T(256)S(1)} %get-tuple-element.5, s32[1000]{0:T(1024)S(1)} %iota_add_fusion), kind=kOutput, calls=%fused_computation.22 | convolution fusion | flops 2361600000 | bytes 14964640 | tf_op jit(solution)/shard_map/dot_general | solution.py:42
  210.1 0.0 reduce-scatter.5.cloned.1.call-update
  210.2 0.2 reduce-scatter.7.cloned.1.call-start
  210.4 10.7 %fusion.15 = f32[1000,4608]{1,0:T(8,128)} fusion(bf16[256,4608]{1,0:T(8,128)(2,1)} %all-gather.5.cloned.1.call-done, f32[256,1000]{0,1:T(8,128)S(1)} %get-tuple-element.9, f32[256]{0:T(256)S(1)} %get-tuple-element.8, s32[256]{0:T(256)S(1)} %get-tuple-element.5, s32[1000]{0:T(1024)S(1)} %iota_add_fusion), kind=kOutput, calls=%fused_computation.21 | convolution fusion | flops 2361600000 | bytes 21821344 | tf_op jit(solution)/shard_map/dot_general | solution.py:50
  221.1 0.0 all-gather.7.cloned.1.call-done
  221.1 12.4 %multiply_add_fusion = f32[1000,4608]{1,0:T(8,128)} fusion(f32[1000,4608]{1,0:T(8,128)} %fusion.15, bf16[256,4608]{1,0:T(8,128)(2,1)} %all-gather.7.cloned.1.call-done, s32[256]{0:T(256)S(1)} %get-tuple-element.6, s32[1000]{0:T(1024)S(1)} %iota_add_fusion), kind=kOutput, calls=%fused_computation.1 | convolution fusion | flops 2368768000 | bytes 39228320 | tf_op jit(solution)/shard_map/dot_general | solution.py:53
  233.5 0.0 copy-done
  233.5 14.3 %fusion = f32[1000,256]{1,0:T(8,128)S(1)} fusion(bf16[4608,256]{1,0:T(8,128)(2,1)S(1)} %copy-done, f32[1000,4608]{1,0:T(8,128)} %multiply_add_fusion), kind=kOutput, calls=%fused_computation.2 | convolution fusion | flops 2377728000 | bytes 21815296 | tf_op jit(solution)/shard_map/dot_general | solution.py:62
  247.8 107.2 %reduce-scatter.5.cloned.1.call-done = f32[8,4608]{1,0:T(8,128)} async-done(((f32[256,4608]{1,0:T(8,128)}), f32[8,4608]{1,0:T(8,128)}) %reduce-scatter.5.cloned.1.call-update) | async-done | bytes 147472 | tf_op jit(solution)/shard_map/reduce_scatter | solution.py:41
  355.0 3.0 copy.13
  357.9 0.0 reduce-scatter.7.cloned.1.call-update
  358.0 9.8 %fusion.5 = f32[1000,256]{1,0:T(8,128)} fusion(f32[1000,256]{1,0:T(8,128)S(1)} %fusion, bf16[4608,256]{1,0:T(8,128)(2,1)S(1)} %copy-done, f32[1000,4608]{1,0:T(8,128)} %multiply_add_fusion), kind=kOutput, calls=%fused_computation.8 | convolution fusion | flops 2364160000 | bytes 22839296 | tf_op jit(solution)/shard_map/dot_general | solution.py:62
  367.7 0.6 dynamic_slice.3
  368.3 90.3 %reduce-scatter.7.cloned.1.call-done = f32[576,8]{1,0:T(8,128)} async-done(((f32[4608,8]{1,0:T(8,128)}), f32[576,8]{1,0:T(8,128)}) %reduce-scatter.7.cloned.1.call-update) | async-done | bytes 18448
  458.6 1.7 copy.14
  (6 shorter events, 0.0 us)
Async XLA Ops:
  7.2 226.3 %copy-start = (bf16[4608,256]{1,0:T(8,128)(2,1)S(1)}, bf16[4608,256]{1,0:T(8,128)(2,1)}, u32[]{:S(2)}) copy-start(bf16[4608,256]{1,0:T(8,128)(2,1)} %param.11) | copy-start | bytes 7077892
  7.2 110.1 %all-gather.5.cloned.1.call-start = ((), (), s32[]{:S(2)}) async-start(), calls=%async_computation.2 | async-start | bytes 2433024 | tf_op jit(solution)/shard_map/all_gather | solution.py:18
  48.9 172.2 %all-gather.7.cloned.1.call-start = ((), (), s32[]{:S(2)}) async-start(), calls=%async_computation.4 | async-start | bytes 2433024 | tf_op jit(solution)/shard_map/all_gather | solution.py:19
  88.0 267.0 %reduce-scatter.5.cloned.1.call-start = ((), (), s32[]{:S(2)}) async-start(), calls=%async_computation.3 | async-start | bytes 4866048 | tf_op jit(solution)/shard_map/reduce_scatter | solution.py:41
  210.2 248.4 %reduce-scatter.7.cloned.1.call-start = ((), (), s32[]{:S(2)}) async-start(), calls=%async_computation.5 | async-start | bytes 2654208
Sparse Core Ops, SparseCore 0:
  49.0 68.2 all-gather.4
  119.2 59.7 all-gather.6
  210.3 144.6 reduce-scatter.4
  358.9 99.6 reduce-scatter.6
where the time goes:
time: 468 us; the launch traced here: 467 us
  waiting for transfers between devices  198 us (42%)
  blocking collectives  182 us (39%)
  matrix products  61.9 us (13%)
  between operations  14.5 us (3%)
  local copies, waits for them, and re-layouts  9.71 us (2%)
    reduce_scatter x1, waiting for transfers between devices, per_device(): lax.psum_scatter(jnp.dot(dlogit, table, preferred_element_type=jnp.float3...  107 us
    unnamed x5, waiting for transfers between devices  90.4 us
    psum x1, blocking collectives, per_device(): total, picked = lax.psum((local_total, local_pick), ('vocab', 'section'))  78.1 us
    all_gather x1, blocking collectives, per_device(): lax.all_gather(hidden, 'section', axis=1, tiled=True)  40.9 us
    all_gather x1, blocking collectives, per_device(): lax.all_gather(input_grad, 'section', axis=1, tiled=True)  38.3 us
    unnamed x1, blocking collectives  25 us
    dot_general x1, matrix products, per_device(): jnp.dot(lower_part, projection, preferred_element_type=jnp.float32)  14.3 us
    dot_general x1, matrix products, per_device(): lax.dot_general(id_hit.astype(jnp.bfloat16), input_all, (((0,), (0,)), ((...  12.4 us
  transfers between devices with their start and end apart: 4, of which 3 were waited for; matrix products, arithmetic and copies ran while one was open for 14% of the time, Pallas kernels for 0%

commit v1 on v0

v1 whole, which is shorter than its diff:
```python
import math

import jax
import jax.numpy as jnp
from jax import lax
from jax.experimental import pallas as pl
from jax.experimental.pallas import tpu as pltpu
from jax.sharding import PartitionSpec as P

MESH = pl.DeviceIdType.MESH
F32 = jnp.float32
BF16 = jnp.bfloat16
NY = 4
NX = 4
NZ = 8
QUARTER = 1152
SECT = 576
PADDED = 640
ROWS = 1000
RANK = 256


def kernel(
    hidden_ref,
    table_hbm,
    ids_ref,
    targets_ref,
    input_ref,
    proj_hbm,
    loss_ref,
    grad_ref,
    low_ref,
    table,
    proj,
    zraw,
    zip_,
    hall,
    ipall,
    idbuf,
    arbuf,
    capped_s,
    expo_s,
    dmat,
    sib_out,
    sib_in,
    acc,
    w0,
    out1a,
    in1a,
    out1b,
    in1b,
    out2,
    in2,
    out3,
    in3,
    load_sem,
    zs,
    zr,
    ids_s,
    ids_r,
    ars,
    arr,
    ags,
    agr,
    css,
    csr,
    ips,
    ipr,
    ics,
    icr,
    xs,
    xr,
    r1s,
    r1r,
    r2s,
    r2r,
    r3s,
    r3r,
):
    sec = lax.axis_index("section")
    voc = lax.axis_index("vocab")
    y = sec // 2
    x = voc // 8
    z = (sec % 2) * 4 + (voc // 2) % 4
    c = voc % 2

    def dev(px, py, pz, pc):
        return {"section": py * 2 + pz // 4, "vocab": (px * 4 + pz % 4) * 2 + pc}

    zc = [
        dev(x, y, (z + dz) % NZ, (c + dc) % 2)
        for dc in range(2)
        for dz in range(NZ)
        if dz or dc
    ]
    xy = [
        dev((x + dx) % NX, (y + dy) % NY, z, c)
        for dx in range(NX)
        for dy in range(NY)
        if dx or dy
    ]
    sibling = dev(x, y, z, (c + 1) % 2)

    def send(src, dst, ssem, rsem, to):
        copy = pltpu.make_async_remote_copy(
            src_ref=src,
            dst_ref=dst,
            send_sem=ssem,
            recv_sem=rsem,
            device_id=to,
            device_id_type=MESH,
        )
        copy.start()
        return copy

    sent = []

    load_table = pltpu.make_async_copy(table_hbm, table, load_sem.at[0])
    load_table.start()
    load_proj = pltpu.make_async_copy(proj_hbm, proj, load_sem.at[1])
    load_proj.start()

    half, zz = (z % 4) // 2, z % 2
    base = half * 64 + x * 16 + zz * 8
    lane = lax.broadcasted_iota(jnp.int32, (1, 256), 1)
    tvec = jnp.zeros((1, 256), jnp.int32)
    ivec = jnp.zeros((1, 256), jnp.int32)
    for i in range(8):
        here = lane == base + i
        tvec = jnp.where(here, targets_ref[i], tvec)
        ivec = jnp.where(here, ids_ref[i], ivec)
    mine = sec == 0
    idbuf[0, :, 0:256] = jnp.where(mine, tvec, 0).astype(F32)
    idbuf[0, :, 256:512] = jnp.where(mine, ivec, 0).astype(F32)
    zraw[z, :, 0:SECT] = hidden_ref[...].astype(F32)

    barrier = pltpu.get_barrier_semaphore()
    for peer in zc + xy:
        pl.semaphore_signal(barrier, inc=1, device_id=peer, device_id_type=MESH)
    pl.semaphore_wait(barrier, len(zc) + len(xy))

    zcopies = [
        send(zraw.at[z], zraw.at[z], zs.at[dz - 1], zr.at[dz - 1], dev(x, y, (z + dz) % NZ, c))
        for dz in range(1, NZ)
    ]

    def swap(v):
        return jnp.concatenate(
            [v[:, 128:256], v[:, 0:128], v[:, 384:512], v[:, 256:384]], axis=1
        )

    def fold_zc(buf):
        same = jnp.sum(buf[0:8], axis=0)
        other = jnp.sum(buf[8:16], axis=0)
        return same + swap(other)

    id1 = [
        send(idbuf.at[0], idbuf.at[1 + i], ids_s.at[i], ids_r.at[i], p) for i, p in enumerate(zc)
    ]

    load_proj.wait()
    share = jnp.dot(
        input_ref[...], proj[pl.ds(pl.multiple_of(sec * SECT, 64), SECT), :], preferred_element_type=F32
    )
    zip_[z] = share

    for cp in zcopies:
        cp.wait_recv()
    for h in range(2):
        rows = []
        for k in range(2):
            zl = 2 * h + k
            rows.append(
                jnp.concatenate([zraw[zl][:, 0:SECT], zraw[zl + 4][:, 0:SECT]], axis=1)
            )
        hall[0, h, y, x] = jnp.concatenate(rows, axis=0).astype(BF16)

    stage2 = []
    for d in range(1, 4):
        px = dev((x + d) % NX, y, z, c)
        py = dev(x, (y + d) % NY, z, c)
        stage2.append(send(hall.at[0, 0, y, x], hall.at[0, 0, y, x], ags.at[d - 1], agr.at[d - 1], px))
        stage2.append(send(hall.at[0, 1, y, x], hall.at[0, 1, y, x], ags.at[d + 2], agr.at[d + 2], py))
    ipz = [
        send(zip_.at[z], zip_.at[z], ips.at[dz - 1], ipr.at[dz - 1], dev(x, y, (z + dz) % NZ, c))
        for dz in range(1, NZ)
    ]
    for cp in id1:
        cp.wait_recv()
    idbuf[16] = fold_zc(idbuf)
    id2 = [
        send(idbuf.at[16], idbuf.at[17 + i], ids_s.at[15 + i], ids_r.at[15 + i], p)
        for i, p in enumerate(xy)
    ]
    for cp in stage2:
        cp.wait_recv()
    stage3 = []
    for d in range(1, 4):
        px = dev((x + d) % NX, y, z, c)
        py = dev(x, (y + d) % NY, z, c)
        stage3.append(send(hall.at[0, 0, y], hall.at[0, 0, y], ags.at[d + 5], agr.at[d + 5], py))
        stage3.append(send(hall.at[0, 1, :, x], hall.at[0, 1, :, x], ags.at[d + 8], agr.at[d + 8], px))

    def to_sibling(k):
        fy, fx = (y + 4 - k) % 4, (x + 4 - k) % 4
        return [
            send(hall.at[0, 0, fy], hall.at[1, 0, fy], css.at[2 * k], csr.at[2 * k], sibling),
            send(hall.at[0, 1, :, fx], hall.at[1, 1, :, fx], css.at[2 * k + 1], csr.at[2 * k + 1], sibling),
        ]

    cross = to_sibling(0)
    for cp in ipz:
        cp.wait_recv()
    for h in range(2):
        block = jnp.concatenate(
            [zip_[2 * h] + zip_[2 * h + 4], zip_[2 * h + 1] + zip_[2 * h + 5]], axis=0
        )
        ipall[0, h, y, x] = block.astype(BF16)
    for cp in id2:
        cp.wait_recv()
    idvec = jnp.sum(idbuf[16:32], axis=0)
    targets = idvec[:, 0:256].astype(jnp.int32)
    ids = idvec[:, 256:512].astype(jnp.int32)

    for d in range(1, 4):
        stage3[2 * d - 2].wait_recv()
        stage3[2 * d - 1].wait_recv()
        cross += to_sibling(d)
    for cp in cross:
        cp.wait_recv()
    load_table.wait()

    ip2 = []
    for d in range(1, 4):
        px = dev((x + d) % NX, y, z, c)
        py = dev(x, (y + d) % NY, z, c)
        ip2.append(send(ipall.at[0, 0, y, x], ipall.at[0, 0, y, x], ips.at[d + 6], ipr.at[d + 6], px))
        ip2.append(send(ipall.at[0, 1, y, x], ipall.at[0, 1, y, x], ips.at[d + 9], ipr.at[d + 9], py))

    def tokens_of(ref, yy, width):
        return jnp.concatenate(
            [ref[p, h, yy].reshape(64, width) for p in range(2) for h in range(2)], axis=0
        )

    raw = jnp.zeros((ROWS, 256), F32)
    for yy in range(4):
        raw += lax.dot_general(
            table[:, yy * QUARTER : (yy + 1) * QUARTER],
            tokens_of(hall, yy, QUARTER),
            (((1,), (1,)), ((), ())),
            preferred_element_type=F32,
        )
    capped = 30.0 * jnp.tanh(raw / 30.0)
    expo = jnp.exp(capped)
    offset = (voc * 8 + sec) * ROWS
    row = offset + lax.broadcasted_iota(jnp.int32, (ROWS, 256), 0)
    hit = row == targets
    capped_s[...] = capped
    expo_s[...] = expo
    arbuf[0, :, 0:256] = jnp.sum(expo, axis=0, keepdims=True)
    arbuf[0, :, 256:512] = jnp.sum(jnp.where(hit, capped, 0.0), axis=0, keepdims=True)
    ar1 = [
        send(arbuf.at[0], arbuf.at[1 + i], ars.at[i], arr.at[i], p) for i, p in enumerate(zc)
    ]
    for cp in ip2:
        cp.wait_recv()
    ip3 = []
    for d in range(1, 4):
        px = dev((x + d) % NX, y, z, c)
        py = dev(x, (y + d) % NY, z, c)
        ip3.append(send(ipall.at[0, 0, y], ipall.at[0, 0, y], ips.at[d + 12], ipr.at[d + 12], py))
        ip3.append(send(ipall.at[0, 1, :, x], ipall.at[0, 1, :, x], ips.at[d + 15], ipr.at[d + 15], px))
    for cp in ar1:
        cp.wait_recv()
    arbuf[16] = fold_zc(arbuf)
    ar2 = [
        send(arbuf.at[16], arbuf.at[17 + i], ars.at[15 + i], arr.at[15 + i], p)
        for i, p in enumerate(xy)
    ]
    hproj = jnp.zeros((256, RANK), F32)
    for yy in range(4):
        hproj += jnp.dot(
            tokens_of(hall, yy, QUARTER),
            proj[yy * QUARTER : (yy + 1) * QUARTER, :],
            preferred_element_type=F32,
        )
    for cp in ar2:
        cp.wait_recv()
    sums = jnp.sum(arbuf[16:32], axis=0)
    total, picked = sums[:, 0:256], sums[:, 256:512]
    loss = jnp.log(total) - picked
    column = lax.broadcasted_iota(jnp.int32, (8, 256), 1)
    spot = base + lax.broadcasted_iota(jnp.int32, (8, 256), 0)
    loss_ref[...] = jnp.sum(jnp.where(column == spot, loss, 0.0), axis=1, keepdims=True)

    capped = capped_s[...]
    dlogit_t = (
        (expo_s[...] / total - (row == targets).astype(F32)) * (1.0 - (capped / 30.0) ** 2)
    ).astype(BF16)
    dmat[...] = dlogit_t.T

    cross_out = []
    for k in range(4):
        yy = (y + (2, 1, 3, 0)[k]) % 4
        part = jnp.dot(
            dmat[...],
            table[:, pl.ds(pl.multiple_of(yy * QUARTER, 128), QUARTER)],
            preferred_element_type=F32,
        )
        sib_out[k] = part[128:256].astype(BF16).reshape(2, 4, 16, QUARTER)
        cross_out.append(send(sib_out.at[k], sib_in.at[k], xs.at[k], xr.at[k], sibling))
        acc[k] = part[0:128].reshape(2, 4, 16, QUARTER)
    first = []
    for k in range(4):
        dy = (2, 1, 3, 0)[k]
        cross_out[k].wait_recv()
        acc[k] = acc[k] + sib_in[k].astype(F32)
        if dy:
            out1a[k] = acc[k, 0].astype(BF16)
            first.append(send(out1a.at[k], in1a.at[k], r1s.at[k], r1r.at[k], dev(x, (y + dy) % NY, z, c)))
        for d in range(1, 4):
            xx = (x + d) % NX
            out1b[k, d - 1] = acc[k, 1, xx].astype(BF16)
            slot = 2 + 3 * k + d
            first.append(
                send(out1b.at[k, d - 1], in1b.at[k, d - 1], r1s.at[slot], r1r.at[slot], dev(xx, y, z, c))
            )

    for cp in ip3:
        cp.wait_recv()
    icross = []
    for k in range(4):
        fy = (y + 4 - k) % 4
        icross.append(send(ipall.at[0, 0, fy], ipall.at[1, 0, fy], ics.at[2 * k], icr.at[2 * k], sibling))
        fx = (x + 4 - k) % 4
        icross.append(
            send(ipall.at[0, 1, :, fx], ipall.at[1, 1, :, fx], ics.at[2 * k + 1], icr.at[2 * k + 1], sibling)
        )

    for cp in first:
        cp.wait_recv()
    w0[...] = acc[3, 0]
    for k in range(3):
        w0[...] = w0[...] + in1a[k].astype(F32)
    second = []
    for d in range(1, 4):
        xx = (x + d) % NX
        out2[0, d - 1] = w0[xx].astype(BF16)
        second.append(send(out2.at[0, d - 1], in2.at[0, d - 1], r2s.at[d - 1], r2r.at[d - 1], dev(xx, y, z, c)))
    for k in range(4):
        w1 = acc[k, 1, x]
        for d in range(3):
            w1 = w1 + in1b[k, d].astype(F32)
        if k < 3:
            dy = (2, 1, 3)[k]
            out2[1, k] = w1.astype(BF16)
            second.append(
                send(out2.at[1, k], in2.at[1, k], r2s.at[3 + k], r2r.at[3 + k], dev(x, (y + dy) % NY, z, c))
            )

    def split(v):
        upper = v.astype(BF16)
        return upper, (v - upper.astype(F32)).astype(BF16)

    for cp in icross:
        cp.wait_recv()
    hp_hi, hp_lo = split(hproj)
    iproj = tokens_of(ipall, 0, RANK).astype(F32)
    for yy in range(1, 4):
        iproj = iproj + tokens_of(ipall, yy, RANK).astype(F32)
    ip_hi, ip_lo = split(iproj * math.sqrt(NY * QUARTER))
    picks = (row == ids).astype(BF16)
    low_ref[...] = (
        jnp.dot(dlogit_t, hp_hi, preferred_element_type=F32)
        + jnp.dot(dlogit_t, hp_lo, preferred_element_type=F32)
        + jnp.dot(picks, ip_hi, preferred_element_type=F32)
        + jnp.dot(picks, ip_lo, preferred_element_type=F32)
    )

    for cp in second:
        cp.wait_recv()
    halves = []
    own0 = w0[x]
    for d in range(3):
        own0 = own0 + in2[0, d].astype(F32)
        w1 = w1 + in2[1, d].astype(F32)
    halves = (own0, w1)
    for zl in range(4):
        block = halves[zl // 2][8 * (zl % 2) : 8 * (zl % 2) + 8]
        out3[zl, :, 0:SECT] = block[:, 0:SECT]
        out3[zl + 4, :, 0:SECT] = block[:, SECT:QUARTER]
    third = [
        send(out3.at[(z + dz) % NZ], in3.at[z], r3s.at[dz - 1], r3r.at[dz - 1], dev(x, y, (z + dz) % NZ, c))
        for dz in range(1, NZ)
    ]
    in3[z] = out3[z]
    for cp in third:
        cp.wait_recv()
    grad = in3[0]
    for k in range(1, NZ):
        grad = grad + in3[k]
    grad_ref[...] = grad[:, 0:SECT].astype(BF16)
    for group in (
        zcopies, id1, stage2, ipz, id2, stage3, cross, ip2, ar1, ip3, ar2, cross_out, first, icross, second, third
    ):
        for cp in group:
            cp.wait_send()


def per_device(hidden, table, token_ids, targets, input_grad, projection):
    dma = pltpu.SemaphoreType.DMA
    vmem = pl.BlockSpec(memory_space=pltpu.VMEM)
    smem = pl.BlockSpec(memory_space=pltpu.SMEM)
    hbm = pl.BlockSpec(memory_space=pl.ANY)
    loss, grad, low = pl.pallas_call(
        kernel,
        out_shape=(
            jax.ShapeDtypeStruct((8, 1), F32),
            jax.ShapeDtypeStruct((8, SECT), BF16),
            jax.ShapeDtypeStruct((ROWS, RANK), F32),
        ),
        in_specs=[vmem, hbm, smem, smem, vmem, hbm],
        out_specs=(vmem, vmem, vmem),
        scratch_shapes=[
            pltpu.VMEM((ROWS, NY * QUARTER), BF16),
            pltpu.VMEM((NY * QUARTER, RANK), BF16),
            pltpu.VMEM((NZ, 8, PADDED), F32),
            pltpu.VMEM((NZ, 8, RANK), F32),
            pltpu.VMEM((2, 2, NY, NX, 16, QUARTER), BF16),
            pltpu.VMEM((2, 2, NY, NX, 16, RANK), BF16),
            pltpu.VMEM((32, 1, 512), F32),
            pltpu.VMEM((32, 1, 512), F32),
            pltpu.VMEM((ROWS, 256), F32),
            pltpu.VMEM((ROWS, 256), F32),
            pltpu.VMEM((256, ROWS), BF16),
            pltpu.VMEM((4, 2, NX, 16, QUARTER), BF16),
            pltpu.VMEM((4, 2, NX, 16, QUARTER), BF16),
            pltpu.VMEM((4, 2, NX, 16, QUARTER), F32),
            pltpu.VMEM((NX, 16, QUARTER), F32),
            pltpu.VMEM((3, NX, 16, QUARTER), BF16),
            pltpu.VMEM((3, NX, 16, QUARTER), BF16),
            pltpu.VMEM((4, 3, 16, QUARTER), BF16),
            pltpu.VMEM((4, 3, 16, QUARTER), BF16),
            pltpu.VMEM((2, 3, 16, QUARTER), BF16),
            pltpu.VMEM((2, 3, 16, QUARTER), BF16),
            pltpu.VMEM((NZ, 8, PADDED), F32),
            pltpu.VMEM((NZ, 8, PADDED), F32),
            dma((2,)),
            dma((7,)), dma((7,)),
            dma((30,)), dma((30,)),
            dma((30,)), dma((30,)),
            dma((12,)), dma((12,)),
            dma((8,)), dma((8,)),
            dma((19,)), dma((19,)),
            dma((8,)), dma((8,)),
            dma((4,)), dma((4,)),
            dma((15,)), dma((15,)),
            dma((6,)), dma((6,)),
            dma((7,)), dma((7,)),
        ],
        compiler_params=pltpu.CompilerParams(
            collective_id=0, has_side_effects=True, vmem_limit_bytes=58 * 2**20
        ),
        cost_estimate=pl.CostEstimate(flops=6 * 10**9, bytes_accessed=13 * 10**6, transcendentals=512000),
    )(hidden, table, token_ids, targets, input_grad, projection)
    return loss.reshape(8), grad, low


def solution(mesh):
    placed = (
        P("vocab", "section"),
        P(("vocab", "section"), None),
        P("vocab"),
        P("vocab"),
        P("vocab", "section"),
        P(),
    )
    return jax.shard_map(
        per_device,
        mesh=mesh,
        in_specs=placed,
        out_specs=(P("vocab"), P("vocab", "section"), P(("vocab", "section"), None)),
        check_vma=False,
    )
```

time: 468 us -> 82.2 us (0.18)
  waiting for transfers between devices: 198 us -> 0 us
  blocking collectives: 182 us -> 0 us
  Pallas kernels: 0 us -> 76.4 us
  matrix products: 61.9 us -> 0 us
  between operations: 14.5 us -> 0.64 us
  local copies, waits for them, and re-layouts: 9.71 us -> 3.54 us
    reduce_scatter x1 -> x0, waiting for transfers between devices: 107 us -> none  [per_device(): lax.psum_scatter(jnp.dot(dlogit, table, preferred_element_type=jnp.float3...]
    unnamed x5 -> x0, waiting for transfers between devices: 90.4 us -> none
    all_gather x2 -> x0, blocking collectives: 79.1 us -> none  [the longest x1 40.9 us: per_device(): lax.all_gather(hidden, 'section', axis=1, tiled=True)]
    psum x1 -> x0, blocking collectives: 78.1 us -> none  [per_device(): total, picked = lax.psum((local_total, local_pick), ('vocab', 'section'))]
    pallas_call x0 -> x1, Pallas kernels: none -> 76.4 us  [per_device(): pl.pallas_call(kernel, out_shape=(jax.ShapeDtypeStruct((8, 1), F32), jax....]
    dot_general x6 -> x0, matrix products: 61.9 us -> none  [the longest x1 14.3 us: per_device(): jnp.dot(lower_part, projection, preferred_element_type=jnp.float32)]
    unnamed x1 -> x0, blocking collectives: 25 us -> none
    unnamed x11 -> x2, local copies, waits for them, and re-layouts: 9.1 us -> 3.54 us
  transfers between devices with their start and end apart: 4 -> 0, of which waited for: 3 -> 0; matrix products, arithmetic and copies ran while one was open for 14% -> 0% of each run, Pallas kernels for 0% -> 0%
where the time goes in v1:
time: 82.2 us; the launch traced here: 81.9 us
  Pallas kernels  76.4 us (93%)
  local copies, waits for them, and re-layouts  3.54 us (4%)
  other arithmetic  1.3 us (2%)
    pallas_call x1, Pallas kernels, per_device(): pl.pallas_call(kernel, out_shape=(jax.ShapeDtypeStruct((8, 1), F32), jax....  76.4 us
    unnamed x2, local copies, waits for them, and re-layouts  3.54 us

profile of v1, /device:TPU:1, one launch (start us, length us, event | category | flops | bytes accessed | tf_op | source)
XLA Modules:
  0.0 81.9 jit_solution(15162745628238837974)
XLA Ops:
  0.6 76.4 %shard_map.85 = (f32[8,1]{1,0:T(8,128)}, bf16[8,576]{1,0:T(8,128)(2,1)}, f32[1000,256]{1,0:T(8,128)}) custom-call(bf16[8,576]{1,0:T(8,128)(2,1)} %hidden_ref.1, bf16[1000,4608]{1,0:T(8,128)(2,1)} %table_hbm.1, s32[8]{0:T(128)} %ids_ref.1, s32[8]{0:T(128)} %targets_ref.1, bf16[8,576]{1,0:T(8,128)(2,1)} %input_ref.1, bf16[4608,256]{1,0:T(8,128)(2,1)} %proj_hbm.1), custom_call_target="tpu_custom_call" | custom-call | flops 6000000000 | bytes 13000000 | tf_op jit(solution)/shard_map/pallas_call | solution.py:415
  77.0 1.3 %reduce = f32[8]{0:T(128)} reduce(f32[8,1]{1,0:T(8,128)} %get-tuple-element.6, f32[]{:T(128)} %constant.5), dimensions={1}, to_apply=%get-tuple-element.6.reduce_sub_computation | reduce | bytes 68 | tf_op jit(solution)/shard_map/pallas_call | solution.py:415
  78.3 1.3 %copy.11 = bf16[8,576]{1,0:T(8,128)(2,1)} copy(bf16[8,576]{1,0:T(8,128)(2,1)} %get-tuple-element.13) | data formatting | bytes 18432
  79.6 2.2 %copy.12 = f32[1000,256]{1,0:T(8,128)} copy(f32[1000,256]{1,0:T(8,128)} %get-tuple-element.14) | data formatting | bytes 2048000

commit v2 on v1

v2 whole, which is shorter than its diff:
```python
import math

import jax
import jax.numpy as jnp
from jax import lax
from jax.experimental import pallas as pl
from jax.experimental.pallas import tpu as pltpu
from jax.sharding import PartitionSpec as P

MESH = pl.DeviceIdType.MESH
F32 = jnp.float32
BF16 = jnp.bfloat16
NY = 4
NX = 4
NZ = 8
QUARTER = 1152
SECT = 576
PIECE = 288
ROWS = 1000
RANK = 256
FAR = (2, 1, 3, 0)


def kernel(
    hidden_ref,
    table_hbm,
    ids_ref,
    targets_ref,
    input_ref,
    proj_hbm,
    loss_ref,
    grad_ref,
    low_ref,
    table,
    proj,
    zraw,
    ipz,
    hall,
    ipy,
    ipx,
    idbuf,
    arbuf,
    capped_s,
    expo_s,
    dmat,
    scale,
    sib_out,
    sib_in,
    acc,
    tsib_out,
    tsib_in,
    tacc,
    tin0,
    tin1,
    out1a,
    in1a,
    out1b,
    in1b,
    out2,
    in2,
    out3,
    in3,
    load_sem,
    zs,
    zr,
    ids_s,
    ids_r,
    ars,
    arr,
    ags,
    agr,
    css,
    csr,
    ips,
    ipr,
    xs,
    xr,
    txs,
    txr,
    ts,
    tr,
    r1s,
    r1r,
    r2s,
    r2r,
    r3s,
    r3r,
):
    sec = lax.axis_index("section")
    voc = lax.axis_index("vocab")
    y = sec // 2
    x = voc // 8
    z = (sec % 2) * 4 + (voc // 2) % 4
    c = voc % 2

    def dev(px, py, pz, pc):
        return {"section": py * 2 + pz // 4, "vocab": (px * 4 + pz % 4) * 2 + pc}

    zc = [
        dev(x, y, (z + dz) % NZ, (c + dc) % 2)
        for dc in range(2)
        for dz in range(NZ)
        if dz or dc
    ]
    xy = [
        dev((x + dx) % NX, (y + dy) % NY, z, c)
        for dx in range(NX)
        for dy in range(NY)
        if dx or dy
    ]
    sibling = dev(x, y, z, (c + 1) % 2)

    def xpeer(d):
        return dev((x + d) % NX, y, z, c)

    def ypeer(d):
        return dev(x, (y + d) % NY, z, c)

    def zpeer(d):
        return dev(x, y, (z + d) % NZ, c)

    started = []

    def send(src, dst, sems, slot, to):
        copy = pltpu.make_async_remote_copy(
            src_ref=src,
            dst_ref=dst,
            send_sem=sems[0].at[slot],
            recv_sem=sems[1].at[slot],
            device_id=to,
            device_id_type=MESH,
        )
        copy.start()
        started.append(copy)
        return copy

    def arrive(copies):
        for copy in copies:
            copy.wait_recv()

    load_table = pltpu.make_async_copy(table_hbm, table, load_sem.at[0])
    load_table.start()
    load_proj = pltpu.make_async_copy(proj_hbm, proj, load_sem.at[1])
    load_proj.start()

    half, zz = (z % 4) // 2, z % 2
    base = half * 64 + x * 16 + zz * 8
    lane = lax.broadcasted_iota(jnp.int32, (1, 256), 1)
    tvec = jnp.zeros((1, 256), jnp.int32)
    ivec = jnp.zeros((1, 256), jnp.int32)
    for i in range(8):
        here = lane == base + i
        tvec = jnp.where(here, targets_ref[i], tvec)
        ivec = jnp.where(here, ids_ref[i], ivec)
    mine = sec == 0
    idbuf[0, :, 0:256] = jnp.where(mine, tvec, 0).astype(F32)
    idbuf[0, :, 256:512] = jnp.where(mine, ivec, 0).astype(F32)

    def pack(v):
        return jnp.concatenate([v[:, 0:PIECE], v[:, PIECE:SECT]], axis=0)

    def unpack(v):
        return jnp.concatenate([v[0:8, 0:PIECE], v[8:16, 0:PIECE]], axis=1)

    zraw[z, :, 0:PIECE] = pack(hidden_ref[...].astype(F32)).astype(BF16)

    barrier = pltpu.get_barrier_semaphore()
    for peer in zc + xy:
        pl.semaphore_signal(barrier, inc=1, device_id=peer, device_id_type=MESH)
    pl.semaphore_wait(barrier, len(zc) + len(xy))

    zcopies = [send(zraw.at[z], zraw.at[z], (zs, zr), d - 1, zpeer(d)) for d in range(1, NZ)]

    def swap(v):
        return jnp.concatenate(
            [v[:, 128:256], v[:, 0:128], v[:, 384:512], v[:, 256:384]], axis=1
        )

    def sum_zc(buf):
        return jnp.sum(buf[0:8], axis=0) + swap(jnp.sum(buf[8:16], axis=0))

    id1 = [send(idbuf.at[0], idbuf.at[1 + i], (ids_s, ids_r), i, p) for i, p in enumerate(zc)]

    load_proj.wait()
    ipz[z] = jnp.dot(
        input_ref[...],
        proj[pl.ds(pl.multiple_of(sec * SECT, 64), SECT), :],
        preferred_element_type=F32,
    )

    arrive(zcopies)
    for h in range(2):
        rows = []
        for k in range(2):
            zl = 2 * h + k
            low_part = unpack(zraw[zl].astype(F32))
            high_part = unpack(zraw[zl + 4].astype(F32))
            rows.append(jnp.concatenate([low_part, high_part], axis=1))
        hall[0, h, y, x] = jnp.concatenate(rows, axis=0).astype(BF16)

    ag = (ags, agr)
    near = {}
    far = {}

    def spread(j):
        bx, by = (x + 4 - j) % NX, (y + 4 - j) % NY
        for d in (1, 3, 2):
            far[0, j, d] = send(hall.at[0, 0, y, bx], hall.at[0, 0, y, bx], ag, 6 + 3 * j + d - 1, ypeer(d))
            far[1, j, d] = send(hall.at[0, 1, by, x], hall.at[0, 1, by, x], ag, 18 + 3 * j + d - 1, xpeer(d))

    for d in (1, 3, 2):
        near[0, d] = send(hall.at[0, 0, y, x], hall.at[0, 0, y, x], ag, d - 1, xpeer(d))
        near[1, d] = send(hall.at[0, 1, y, x], hall.at[0, 1, y, x], ag, 2 + d, ypeer(d))
    spread(0)
    ip = (ips, ipr)
    ipzc = [send(ipz.at[z], ipz.at[z], ip, d - 1, zpeer(d)) for d in range(1, NZ)]
    arrive(id1)
    idbuf[16] = sum_zc(idbuf)
    for j in (1, 3, 2):
        arrive([near[0, j], near[1, j]])
        spread(j)
    id2 = [
        send(idbuf.at[16], idbuf.at[17 + i], (ids_s, ids_r), 15 + i, p) for i, p in enumerate(xy)
    ]
    arrive(ipzc)
    for h in range(2):
        ipy[y, h] = jnp.concatenate(
            [ipz[2 * h] + ipz[2 * h + 4], ipz[2 * h + 1] + ipz[2 * h + 5]], axis=0
        ).astype(BF16)
    ipyc = [send(ipy.at[y], ipy.at[y], ip, 6 + d, ypeer(d)) for d in range(1, 4)]
    load_table.wait()
    arrive(id2)
    idvec = jnp.sum(idbuf[16:32], axis=0)
    targets = idvec[:, 0:256].astype(jnp.int32)
    ids = idvec[:, 256:512].astype(jnp.int32)
    offset = (voc * 8 + sec) * ROWS
    row = offset + lax.broadcasted_iota(jnp.int32, (ROWS, 256), 0)

    dmat[...] = (row == targets).astype(F32).astype(BF16).T
    tcross = []
    for k in range(4):
        yy = (y + FAR[k]) % NY
        part = jnp.dot(
            dmat[...],
            table[:, pl.ds(pl.multiple_of(yy * QUARTER, 128), QUARTER)],
            preferred_element_type=F32,
        ).astype(BF16)
        tsib_out[k] = part[128:256].reshape(2, NX, 16, QUARTER)
        tcross.append(send(tsib_out.at[k], tsib_in.at[k], (txs, txr), k, sibling))
        tacc[k] = part[0:128].reshape(2, NX, 16, QUARTER)

    cross = []
    for j in (0, 1, 3, 2):
        bx, by = (x + 4 - j) % NX, (y + 4 - j) % NY
        arrive([far[h, j, d] for h in range(2) for d in range(1, 4)])
        cross.append(send(hall.at[0, 0, :, bx], hall.at[1, 0, :, bx], (css, csr), 2 * j, sibling))
        cross.append(send(hall.at[0, 1, by], hall.at[1, 1, by], (css, csr), 2 * j + 1, sibling))

    for k in range(4):
        arrive([tcross[k]])
        tacc[k] = tacc[k] + tsib_in[k]
    tfirst = []
    for k in range(3):
        tfirst.append(send(tacc.at[k, 0], tin0.at[k], (ts, tr), k, ypeer(FAR[k])))
        xx = (x + FAR[k]) % NX
        tfirst.append(send(tacc.at[:, 1, xx], tin1.at[k], (ts, tr), 3 + k, xpeer(FAR[k])))
    arrive(cross)

    def tokens_of(yy):
        return jnp.concatenate(
            [hall[p, h, yy].reshape(64, QUARTER) for p in range(2) for h in range(2)], axis=0
        )

    raw = jnp.zeros((ROWS, 256), F32)
    for yy in range(4):
        raw += lax.dot_general(
            table[:, yy * QUARTER : (yy + 1) * QUARTER],
            tokens_of(yy),
            (((1,), (1,)), ((), ())),
            preferred_element_type=F32,
        )
    capped = 30.0 * jnp.tanh(raw / 30.0)
    expo = jnp.exp(capped)
    hit = row == targets
    capped_s[...] = capped
    expo_s[...] = expo
    arbuf[0, :, 0:256] = jnp.sum(expo, axis=0, keepdims=True)
    arbuf[0, :, 256:512] = jnp.sum(jnp.where(hit, capped, 0.0), axis=0, keepdims=True)
    ar1 = [send(arbuf.at[0], arbuf.at[1 + i], (ars, arr), i, p) for i, p in enumerate(zc)]

    dmat[...] = jnp.where(hit, 0.0, expo * (1.0 - (capped / 30.0) ** 2)).astype(BF16).T
    r1 = (r1s, r1r)
    first0 = {}
    first1 = {}
    crossed = []

    def first_sends(k):
        arrive([crossed[k]])
        acc[k] = acc[k] + sib_in[k].astype(F32)
        for j in range(3):
            dx = FAR[j]
            xx = (x + dx) % NX
            out1b[k, j] = acc[k, 1, xx].astype(BF16)
            first1[k, j] = send(out1b.at[k, j], in1b.at[k, j], r1, 12 + 3 * k + j, xpeer(dx))
            if k < 3:
                out1a[k, j] = acc[k, 0, xx].astype(BF16)
                first0[k, j] = send(out1a.at[k, j], in1a.at[k, j], r1, 4 * k + j, ypeer(FAR[k]))

    for k in range(4):
        yy = (y + FAR[k]) % NY
        part = jnp.dot(
            dmat[...],
            table[:, pl.ds(pl.multiple_of(yy * QUARTER, 128), QUARTER)],
            preferred_element_type=F32,
        )
        sib_out[k] = part[128:256].astype(BF16).reshape(2, NX, 16, QUARTER)
        crossed.append(send(sib_out.at[k], sib_in.at[k], (xs, xr), k, sibling))
        acc[k] = part[0:128].reshape(2, NX, 16, QUARTER)
        if k:
            first_sends(k - 1)
    first_sends(3)
    for k in range(3):
        out1a[k, 3] = acc[k, 0, x].astype(BF16)
        first0[k, 3] = send(out1a.at[k, 3], in1a.at[k, 3], r1, 4 * k + 3, ypeer(FAR[k]))

    arrive(ar1)
    arbuf[16] = sum_zc(arbuf)
    ar2 = [send(arbuf.at[16], arbuf.at[17 + i], (ars, arr), 15 + i, p) for i, p in enumerate(xy)]
    arrive(ipyc)
    ipx[0, x] = (
        ipy[0].astype(F32) + ipy[1].astype(F32) + ipy[2].astype(F32) + ipy[3].astype(F32)
    ).astype(BF16)
    ipxc = [send(ipx.at[0, x], ipx.at[0, x], ip, 9 + d, xpeer(d)) for d in range(1, 4)]
    hproj = jnp.zeros((256, RANK), F32)
    for yy in range(4):
        hproj += jnp.dot(
            tokens_of(yy), proj[yy * QUARTER : (yy + 1) * QUARTER, :], preferred_element_type=F32
        )
    arrive(ar2)
    sums = jnp.sum(arbuf[16:32], axis=0)
    total, picked = sums[:, 0:256], sums[:, 256:512]
    inverse = 1.0 / total
    target_coef = (jnp.exp(picked) / total - 1.0) * (1.0 - (picked / 30.0) ** 2)
    scale[0] = jnp.broadcast_to(inverse[:, 0:128], (128, 128)).T.reshape(2, NX, 16, 128)
    scale[1] = jnp.broadcast_to(target_coef[:, 0:128], (128, 128)).T.reshape(2, NX, 16, 128)

    def scaled(u, t, h, xx):
        return u * scale[0, h, xx][:, 0:1] + t * scale[1, h, xx][:, 0:1]

    arrive(tfirst)
    r2 = (r2s, r2r)
    second = []
    kept = {}

    def step0(j):
        arrive([first0[k, j] for k in range(3)])
        xx = (x + FAR[j]) % NX
        u = acc[3, 0, xx]
        t = tacc[3, 0, xx].astype(F32)
        for k in range(3):
            u = u + in1a[k, j].astype(F32)
            t = t + tin0[k, xx].astype(F32)
        s = scaled(u, t, 0, xx)
        if j < 3:
            out2[0, j] = s.astype(BF16)
            second.append(send(out2.at[0, j], in2.at[0, j], r2, j, xpeer(FAR[j])))
        else:
            kept[0] = s

    def step1(k):
        arrive([first1[k, j] for j in range(3)])
        u = acc[k, 1, x]
        t = tacc[k, 1, x].astype(F32)
        for j in range(3):
            u = u + in1b[k, j].astype(F32)
            t = t + tin1[j, k].astype(F32)
        s = scaled(u, t, 1, x)
        if k < 3:
            out2[1, k] = s.astype(BF16)
            second.append(send(out2.at[1, k], in2.at[1, k], r2, 3 + k, ypeer(FAR[k])))
        else:
            kept[1] = s

    step1(0)
    step1(1)
    step0(0)
    step1(2)
    step0(1)
    step0(2)
    step1(3)
    step0(3)
    arrive(ipxc)
    ipcross = send(ipx.at[0], ipx.at[1], ip, 13, sibling)

    arrive(second)
    for zl in range(4):
        h = zl // 2
        if zl % 2 == 0:
            whole = kept[h]
            for j in range(3):
                whole = whole + in2[h, j].astype(F32)
        block = whole[8 * (zl % 2) : 8 * (zl % 2) + 8]
        out3[zl, :, 0:PIECE] = pack(block[:, 0:SECT]).astype(BF16)
        out3[zl + 4, :, 0:PIECE] = pack(block[:, SECT:QUARTER]).astype(BF16)
    third = [
        send(out3.at[(z + d) % NZ], in3.at[z], (r3s, r3r), d - 1, zpeer(d)) for d in range(1, NZ)
    ]
    in3[z] = out3[z]

    loss = jnp.log(total) - picked
    for i in range(8):
        loss_ref[i] = jnp.sum(jnp.where(lane == base + i, loss, 0.0))

    def split(v):
        upper = v.astype(BF16)
        return upper, (v - upper.astype(F32)).astype(BF16)

    dlogit_t = (
        (expo_s[...] / total - (row == targets).astype(F32)) * (1.0 - (capped_s[...] / 30.0) ** 2)
    ).astype(BF16)
    arrive([ipcross])
    iproj = jnp.concatenate(
        [
            jnp.concatenate([ipx[p, xx, h] for xx in range(NX)], axis=0)
            for p in range(2)
            for h in range(2)
        ],
        axis=0,
    ).astype(F32)
    hp_hi, hp_lo = split(hproj)
    ip_hi, ip_lo = split(iproj * math.sqrt(NY * QUARTER))
    picks = (row == ids).astype(F32).astype(BF16)
    low_ref[...] = (
        jnp.dot(dlogit_t, hp_hi, preferred_element_type=F32)
        + jnp.dot(dlogit_t, hp_lo, preferred_element_type=F32)
        + jnp.dot(picks, ip_hi, preferred_element_type=F32)
        + jnp.dot(picks, ip_lo, preferred_element_type=F32)
    )

    arrive(third)
    grad = in3[0].astype(F32)
    for k in range(1, NZ):
        grad = grad + in3[k].astype(F32)
    grad_ref[...] = unpack(grad).astype(BF16)
    for copy in started:
        copy.wait_send()


def hand_over(loss_in, grad_in, low_in, loss_out, grad_out, low_out):
    low_out[...] = low_in[...]
    grad_out[...] = grad_in[...]
    for i in range(8):
        loss_out[i] = loss_in[i]


def per_device(hidden, table, token_ids, targets, input_grad, projection):
    dma = pltpu.SemaphoreType.DMA
    vmem = pl.BlockSpec(memory_space=pltpu.VMEM)
    smem = pl.BlockSpec(memory_space=pltpu.SMEM)
    hbm = pl.BlockSpec(memory_space=pl.ANY)
    shapes = (
        jax.ShapeDtypeStruct((8,), F32),
        jax.ShapeDtypeStruct((8, SECT), BF16),
        jax.ShapeDtypeStruct((ROWS, RANK), F32),
    )

    def blocks(n, kind=BF16):
        return pltpu.VMEM((n, 2, NX, 16, QUARTER), kind)

    def pairs(*counts):
        return [dma((n,)) for n in counts for _ in range(2)]

    outs = pl.pallas_call(
        kernel,
        out_shape=shapes,
        in_specs=[vmem, hbm, smem, smem, vmem, hbm],
        out_specs=(smem, vmem, vmem),
        scratch_shapes=[
            pltpu.VMEM((ROWS, NY * QUARTER), BF16),
            pltpu.VMEM((NY * QUARTER, RANK), BF16),
            pltpu.VMEM((NZ, 16, 384), BF16),
            pltpu.VMEM((NZ, 8, RANK), F32),
            pltpu.VMEM((2, 2, NY, NX, 16, QUARTER), BF16),
            pltpu.VMEM((NY, 2, 16, RANK), BF16),
            pltpu.VMEM((2, NX, 2, 16, RANK), BF16),
            pltpu.VMEM((32, 1, 512), F32),
            pltpu.VMEM((32, 1, 512), F32),
            pltpu.VMEM((ROWS, 256), F32),
            pltpu.VMEM((ROWS, 256), F32),
            pltpu.VMEM((256, ROWS), BF16),
            pltpu.VMEM((2, 2, NX, 16, 128), F32),
            blocks(4),
            blocks(4),
            blocks(4, F32),
            blocks(4),
            blocks(4),
            blocks(4),
            pltpu.VMEM((3, NX, 16, QUARTER), BF16),
            pltpu.VMEM((3, 4, 16, QUARTER), BF16),
            pltpu.VMEM((3, 4, 16, QUARTER), BF16),
            pltpu.VMEM((3, 4, 16, QUARTER), BF16),
            pltpu.VMEM((4, 3, 16, QUARTER), BF16),
            pltpu.VMEM((4, 3, 16, QUARTER), BF16),
            pltpu.VMEM((2, 3, 16, QUARTER), BF16),
            pltpu.VMEM((2, 3, 16, QUARTER), BF16),
            pltpu.VMEM((NZ, 16, 384), BF16),
            pltpu.VMEM((NZ, 16, 384), BF16),
            dma((2,)),
            *pairs(7, 30, 30, 30, 8, 14, 4, 4, 6, 24, 6, 7),
        ],
        compiler_params=pltpu.CompilerParams(
            collective_id=0, has_side_effects=True, vmem_limit_bytes=58 * 2**20
        ),
        cost_estimate=pl.CostEstimate(
            flops=8 * 10**9, bytes_accessed=13 * 10**6, transcendentals=512000
        ),
    )(hidden, table, token_ids, targets, input_grad, projection)
    return pl.pallas_call(
        hand_over,
        out_shape=shapes,
        in_specs=[smem, vmem, vmem],
        out_specs=(smem, vmem, vmem),
    )(*outs)


def solution(mesh):
    placed = (
        P("vocab", "section"),
        P(("vocab", "section"), None),
        P("vocab"),
        P("vocab"),
        P("vocab", "section"),
        P(),
    )
    return jax.shard_map(
        per_device,
        mesh=mesh,
        in_specs=placed,
        out_specs=(P("vocab"), P("vocab", "section"), P(("vocab", "section"), None)),
        check_vma=False,
    )
```

time: 82.2 us -> 71.9 us (0.87)
  Pallas kernels: 76.4 us -> 71 us
  local copies, waits for them, and re-layouts: 3.54 us -> 0 us
  other arithmetic: 1.3 us -> 0 us
    pallas_call x1 -> x2, Pallas kernels: 76.4 us -> 71 us  [the longest x1 68.7 us: per_device(): pl.pallas_call(kernel, out_shape=shapes, in_specs=[vmem, hbm, smem, smem,...]
    unnamed x2 -> x0, local copies, waits for them, and re-layouts: 3.54 us -> none
    pallas_call x1 -> x0, other arithmetic: 1.3 us -> none  [per_device(): pl.pallas_call(kernel, out_shape=(jax.ShapeDtypeStruct((8, 1), F32), jax....]
where the time goes in v2:
time: 71.9 us; the launch traced here: 71.8 us
  Pallas kernels  71 us (99%)
  between operations  0.8 us (1%)
    pallas_call x1, Pallas kernels, per_device(): pl.pallas_call(kernel, out_shape=shapes, in_specs=[vmem, hbm, smem, smem,...  68.7 us
    pallas_call x1, Pallas kernels, per_device(): pl.pallas_call(hand_over, out_shape=shapes, in_specs=[smem, vmem, vmem],...  2.28 us

profile of v2, /device:TPU:1, one launch (start us, length us, event | category | flops | bytes accessed | tf_op | source)
XLA Modules:
  0.0 71.8 jit_solution(15935495366365004327)
XLA Ops:
  0.6 68.7 %shard_map.85 = (f32[8]{0:T(128)}, bf16[8,576]{1,0:T(8,128)(2,1)}, f32[1000,256]{1,0:T(8,128)}) custom-call(bf16[8,576]{1,0:T(8,128)(2,1)} %hidden_ref.1, bf16[1000,4608]{1,0:T(8,128)(2,1)} %table_hbm.1, s32[8]{0:T(128)} %ids_ref.1, s32[8]{0:T(128)} %targets_ref.1, bf16[8,576]{1,0:T(8,128)(2,1)} %input_ref.1, bf16[4608,256]{1,0:T(8,128)(2,1)} %proj_hbm.1), custom_call_target="tpu_custom_call" | custom-call | flops 8000000000 | bytes 13000000 | tf_op jit(solution)/shard_map/pallas_call | solution.py:473
  69.3 2.3 %shard_map.86 = (f32[8]{0:T(128)}, bf16[8,576]{1,0:T(8,128)(2,1)}, f32[1000,256]{1,0:T(8,128)}) custom-call(f32[8]{0:T(128)} %get-tuple-element.6.loss_in, bf16[8,576]{1,0:T(8,128)(2,1)} %get-tuple-element.7.grad_in, f32[1000,256]{1,0:T(8,128)} %get-tuple-element.8.low_in), custom_call_target="tpu_custom_call" | custom-call | tf_op jit(solution)/shard_map/pallas_call | solution.py:518

commit v3 on v2

--- a/solution.py
+++ b/solution.py
@@ -22,14 +22,19 @@
 
 
 def kernel(
+    hidden_hbm,
+    table_hbm,
+    ids_hbm,
+    targets_hbm,
+    input_hbm,
+    proj_hbm,
+    loss_ref,
+    grad_ref,
+    low_hbm,
     hidden_ref,
-    table_hbm,
     ids_ref,
     targets_ref,
     input_ref,
-    proj_hbm,
-    loss_ref,
-    grad_ref,
     low_ref,
     table,
     proj,
@@ -138,10 +143,23 @@
         for copy in copies:
             copy.wait_recv()
 
+    barrier = pltpu.get_barrier_semaphore()
+    for peer in zc + xy:
+        pl.semaphore_signal(barrier, inc=1, device_id=peer, device_id_type=MESH)
+    load_small = [
+        pltpu.make_async_copy(hidden_hbm, hidden_ref, load_sem.at[2]),
+        pltpu.make_async_copy(input_hbm, input_ref, load_sem.at[3]),
+        pltpu.make_async_copy(ids_hbm, ids_ref, load_sem.at[4]),
+        pltpu.make_async_copy(targets_hbm, targets_ref, load_sem.at[5]),
+    ]
+    for copy in load_small:
+        copy.start()
+    load_proj = pltpu.make_async_copy(proj_hbm, proj, load_sem.at[1])
+    load_proj.start()
     load_table = pltpu.make_async_copy(table_hbm, table, load_sem.at[0])
     load_table.start()
-    load_proj = pltpu.make_async_copy(proj_hbm, proj, load_sem.at[1])
-    load_proj.start()
+    for copy in load_small:
+        copy.wait()
 
     half, zz = (z % 4) // 2, z % 2
     base = half * 64 + x * 16 + zz * 8
@@ -152,7 +170,7 @@
         here = lane == base + i
         tvec = jnp.where(here, targets_ref[i], tvec)
         ivec = jnp.where(here, ids_ref[i], ivec)
-    mine = sec == 0
+    mine = z < 4
     idbuf[0, :, 0:256] = jnp.where(mine, tvec, 0).astype(F32)
     idbuf[0, :, 256:512] = jnp.where(mine, ivec, 0).astype(F32)
 
@@ -164,11 +182,11 @@
 
     zraw[z, :, 0:PIECE] = pack(hidden_ref[...].astype(F32)).astype(BF16)
 
-    barrier = pltpu.get_barrier_semaphore()
-    for peer in zc + xy:
-        pl.semaphore_signal(barrier, inc=1, device_id=peer, device_id_type=MESH)
     pl.semaphore_wait(barrier, len(zc) + len(xy))
 
+    id1 = [
+        send(idbuf.at[0], idbuf.at[d], (ids_s, ids_r), d - 1, xpeer(d)) for d in range(1, NX)
+    ]
     zcopies = [send(zraw.at[z], zraw.at[z], (zs, zr), d - 1, zpeer(d)) for d in range(1, NZ)]
 
     def swap(v):
@@ -179,7 +197,11 @@
     def sum_zc(buf):
         return jnp.sum(buf[0:8], axis=0) + swap(jnp.sum(buf[8:16], axis=0))
 
-    id1 = [send(idbuf.at[0], idbuf.at[1 + i], (ids_s, ids_r), i, p) for i, p in enumerate(zc)]
+    arrive(id1)
+    idbuf[4] = jnp.sum(idbuf[0:4], axis=0)
+    id2 = [
+        send(idbuf.at[4], idbuf.at[5 + i], (ids_s, ids_r), 3 + i, p) for i, p in enumerate(zc)
+    ]
 
     load_proj.wait()
     ipz[z] = jnp.dot(
@@ -214,23 +236,17 @@
     spread(0)
     ip = (ips, ipr)
     ipzc = [send(ipz.at[z], ipz.at[z], ip, d - 1, zpeer(d)) for d in range(1, NZ)]
-    arrive(id1)
-    idbuf[16] = sum_zc(idbuf)
-    for j in (1, 3, 2):
-        arrive([near[0, j], near[1, j]])
-        spread(j)
-    id2 = [
-        send(idbuf.at[16], idbuf.at[17 + i], (ids_s, ids_r), 15 + i, p) for i, p in enumerate(xy)
-    ]
-    arrive(ipzc)
-    for h in range(2):
-        ipy[y, h] = jnp.concatenate(
-            [ipz[2 * h] + ipz[2 * h + 4], ipz[2 * h + 1] + ipz[2 * h + 5]], axis=0
-        ).astype(BF16)
-    ipyc = [send(ipy.at[y], ipy.at[y], ip, 6 + d, ypeer(d)) for d in range(1, 4)]
+    def sum_ipz():
+        arrive(ipzc)
+        for h in range(2):
+            ipy[y, h] = jnp.concatenate(
+                [ipz[2 * h] + ipz[2 * h + 4], ipz[2 * h + 1] + ipz[2 * h + 5]], axis=0
+            ).astype(BF16)
+        return [send(ipy.at[y], ipy.at[y], ip, 6 + d, ypeer(d)) for d in range(1, 4)]
+
     load_table.wait()
     arrive(id2)
-    idvec = jnp.sum(idbuf[16:32], axis=0)
+    idvec = sum_zc(idbuf[4:20])
     targets = idvec[:, 0:256].astype(jnp.int32)
     ids = idvec[:, 256:512].astype(jnp.int32)
     offset = (voc * 8 + sec) * ROWS
@@ -238,7 +254,8 @@
 
     dmat[...] = (row == targets).astype(F32).astype(BF16).T
     tcross = []
-    for k in range(4):
+
+    def target_rows(k):
         yy = (y + FAR[k]) % NY
         part = jnp.dot(
             dmat[...],
@@ -249,16 +266,30 @@
         tcross.append(send(tsib_out.at[k], tsib_in.at[k], (txs, txr), k, sibling))
         tacc[k] = part[0:128].reshape(2, NX, 16, QUARTER)
 
+    target_rows(0)
+    for j in (1, 3, 2):
+        arrive([near[0, j], near[1, j]])
+        spread(j)
+    for k in range(1, 4):
+        target_rows(k)
+
     cross = []
-    for j in (0, 1, 3, 2):
+
+    def group(j):
         bx, by = (x + 4 - j) % NX, (y + 4 - j) % NY
         arrive([far[h, j, d] for h in range(2) for d in range(1, 4)])
         cross.append(send(hall.at[0, 0, :, bx], hall.at[1, 0, :, bx], (css, csr), 2 * j, sibling))
         cross.append(send(hall.at[0, 1, by], hall.at[1, 1, by], (css, csr), 2 * j + 1, sibling))
 
+    group(0)
+    ipyc = sum_ipz()
     for k in range(4):
         arrive([tcross[k]])
         tacc[k] = tacc[k] + tsib_in[k]
+    group(1)
+    group(3)
+    group(2)
+
     tfirst = []
     for k in range(3):
         tfirst.append(send(tacc.at[k, 0], tin0.at[k], (ts, tr), k, ypeer(FAR[k])))
@@ -286,8 +317,6 @@
     expo_s[...] = expo
     arbuf[0, :, 0:256] = jnp.sum(expo, axis=0, keepdims=True)
     arbuf[0, :, 256:512] = jnp.sum(jnp.where(hit, capped, 0.0), axis=0, keepdims=True)
-    ar1 = [send(arbuf.at[0], arbuf.at[1 + i], (ars, arr), i, p) for i, p in enumerate(zc)]
-
     dmat[...] = jnp.where(hit, 0.0, expo * (1.0 - (capped / 30.0) ** 2)).astype(BF16).T
     r1 = (r1s, r1r)
     first0 = {}
@@ -306,26 +335,39 @@
                 out1a[k, j] = acc[k, 0, xx].astype(BF16)
                 first0[k, j] = send(out1a.at[k, j], in1a.at[k, j], r1, 4 * k + j, ypeer(FAR[k]))
 
-    for k in range(4):
+    def columns(k):
         yy = (y + FAR[k]) % NY
-        part = jnp.dot(
-            dmat[...],
-            table[:, pl.ds(pl.multiple_of(yy * QUARTER, 128), QUARTER)],
-            preferred_element_type=F32,
-        )
-        sib_out[k] = part[128:256].astype(BF16).reshape(2, NX, 16, QUARTER)
+        return table[:, pl.ds(pl.multiple_of(yy * QUARTER, 128), QUARTER)]
+
+    def sib_part(k):
+        part = jnp.dot(dmat[128:256], columns(k), preferred_element_type=F32)
+        sib_out[k] = part.astype(BF16).reshape(2, NX, 16, QUARTER)
         crossed.append(send(sib_out.at[k], sib_in.at[k], (xs, xr), k, sibling))
-        acc[k] = part[0:128].reshape(2, NX, 16, QUARTER)
-        if k:
-            first_sends(k - 1)
+
+    def own_part(k):
+        part = jnp.dot(dmat[0:128], columns(k), preferred_element_type=F32)
+        acc[k] = part.reshape(2, NX, 16, QUARTER)
+
+    sib_part(0)
+    ar1 = [send(arbuf.at[0], arbuf.at[1 + i], (ars, arr), i, p) for i, p in enumerate(zc)]
+    own_part(0)
+    sib_part(1)
+    first_sends(0)
+    own_part(1)
+    sib_part(2)
+    first_sends(1)
+    own_part(2)
+    sib_part(3)
+    first_sends(2)
+    arrive(ar1)
+    arbuf[16] = sum_zc(arbuf)
+    ar2 = [send(arbuf.at[16], arbuf.at[17 + i], (ars, arr), 15 + i, p) for i, p in enumerate(xy)]
+    own_part(3)
     first_sends(3)
     for k in range(3):
         out1a[k, 3] = acc[k, 0, x].astype(BF16)
         first0[k, 3] = send(out1a.at[k, 3], in1a.at[k, 3], r1, 4 * k + 3, ypeer(FAR[k]))
 
-    arrive(ar1)
-    arbuf[16] = sum_zc(arbuf)
-    ar2 = [send(arbuf.at[16], arbuf.at[17 + i], (ars, arr), 15 + i, p) for i, p in enumerate(xy)]
     arrive(ipyc)
     ipx[0, x] = (
         ipy[0].astype(F32) + ipy[1].astype(F32) + ipy[2].astype(F32) + ipy[3].astype(F32)
@@ -436,12 +478,15 @@
         + jnp.dot(picks, ip_hi, preferred_element_type=F32)
         + jnp.dot(picks, ip_lo, preferred_element_type=F32)
     )
+    store_low = pltpu.make_async_copy(low_ref, low_hbm, load_sem.at[6])
+    store_low.start()
 
     arrive(third)
     grad = in3[0].astype(F32)
     for k in range(1, NZ):
         grad = grad + in3[k].astype(F32)
     grad_ref[...] = unpack(grad).astype(BF16)
+    store_low.wait()
     for copy in started:
         copy.wait_send()
 
@@ -473,9 +518,14 @@
     outs = pl.pallas_call(
         kernel,
         out_shape=shapes,
-        in_specs=[vmem, hbm, smem, smem, vmem, hbm],
-        out_specs=(smem, vmem, vmem),
+        in_specs=[hbm] * 6,
+        out_specs=(smem, vmem, hbm),
         scratch_shapes=[
+            pltpu.VMEM((8, SECT), BF16),
+            pltpu.SMEM((8,), jnp.int32),
+            pltpu.SMEM((8,), jnp.int32),
+            pltpu.VMEM((8, SECT), BF16),
+            pltpu.VMEM((ROWS, RANK), F32),
             pltpu.VMEM((ROWS, NY * QUARTER), BF16),
             pltpu.VMEM((NY * QUARTER, RANK), BF16),
             pltpu.VMEM((NZ, 16, 384), BF16),
@@ -483,7 +533,7 @@
             pltpu.VMEM((2, 2, NY, NX, 16, QUARTER), BF16),
             pltpu.VMEM((NY, 2, 16, RANK), BF16),
             pltpu.VMEM((2, NX, 2, 16, RANK), BF16),
-            pltpu.VMEM((32, 1, 512), F32),
+            pltpu.VMEM((20, 1, 512), F32),
             pltpu.VMEM((32, 1, 512), F32),
             pltpu.VMEM((ROWS, 256), F32),
             pltpu.VMEM((ROWS, 256), F32),
@@ -505,8 +555,8 @@
             pltpu.VMEM((2, 3, 16, QUARTER), BF16),
             pltpu.VMEM((NZ, 16, 384), BF16),
             pltpu.VMEM((NZ, 16, 384), BF16),
-            dma((2,)),
-            *pairs(7, 30, 30, 30, 8, 14, 4, 4, 6, 24, 6, 7),
+            dma((7,)),
+            *pairs(7, 18, 30, 30, 8, 14, 4, 4, 6, 24, 6, 7),
         ],
         compiler_params=pltpu.CompilerParams(
             collective_id=0, has_side_effects=True, vmem_limit_bytes=58 * 2**20

time: 71.9 us -> 62.3 us (0.87); the launches traced: 71.8 us -> 61.3 us
  Pallas kernels: 71 us -> 60.5 us
    pallas_call x1, Pallas kernels: 68.7 us -> 58.2 us  [per_device(): pl.pallas_call(kernel, out_shape=shapes, in_specs=[hbm] * 6, out_specs=(s...]
where the time goes in v3:
time: 62.3 us; the launch traced here: 61.3 us
  Pallas kernels  60.5 us (97%)
  between operations  0.8 us (1%)
    pallas_call x1, Pallas kernels, per_device(): pl.pallas_call(kernel, out_shape=shapes, in_specs=[hbm] * 6, out_specs=(s...  58.2 us
    pallas_call x1, Pallas kernels, per_device(): pl.pallas_call(hand_over, out_shape=shapes, in_specs=[smem, vmem, vmem],...  2.28 us

profile of v3, /device:TPU:1, one launch (start us, length us, event | category | flops | bytes accessed | tf_op | source)
XLA Modules:
  0.0 61.3 jit_solution(17581664854980842924)
XLA Ops:
  0.6 58.2 %shard_map.85 = (f32[8]{0:T(128)}, bf16[8,576]{1,0:T(8,128)(2,1)}, f32[1000,256]{1,0:T(8,128)}) custom-call(bf16[8,576]{1,0:T(8,128)(2,1)} %hidden_hbm.1, bf16[1000,4608]{1,0:T(8,128)(2,1)} %table_hbm.1, s32[8]{0:T(128)} %ids_hbm.1, s32[8]{0:T(128)} %targets_hbm.1, bf16[8,576]{1,0:T(8,128)(2,1)} %input_hbm.1, bf16[4608,256]{1,0:T(8,128)(2,1)} %proj_hbm.1), custom_call_target="tpu_custom_call" | custom-call | flops 8000000000 | bytes 13000000 | tf_op jit(solution)/shard_map/pallas_call | solution.py:518
  58.9 2.3 %shard_map.86 = (f32[8]{0:T(128)}, bf16[8,576]{1,0:T(8,128)(2,1)}, f32[1000,256]{1,0:T(8,128)}) custom-call(f32[8]{0:T(128)} %get-tuple-element.6.loss_in, bf16[8,576]{1,0:T(8,128)(2,1)} %get-tuple-element.7.grad_in, f32[1000,256]{1,0:T(8,128)} %get-tuple-element.8.low_in), custom_call_target="tpu_custom_call" | custom-call | tf_op jit(solution)/shard_map/pallas_call | solution.py:568

commit v4 on v3

--- a/solution.py
+++ b/solution.py
@@ -19,6 +19,7 @@
 ROWS = 1000
 RANK = 256
 FAR = (2, 1, 3, 0)
+ZFAR = (4, 3, 5, 2, 6, 1, 7)
 
 
 def kernel(
@@ -187,7 +188,7 @@
     id1 = [
         send(idbuf.at[0], idbuf.at[d], (ids_s, ids_r), d - 1, xpeer(d)) for d in range(1, NX)
     ]
-    zcopies = [send(zraw.at[z], zraw.at[z], (zs, zr), d - 1, zpeer(d)) for d in range(1, NZ)]
+    zcopies = [send(zraw.at[z], zraw.at[z], (zs, zr), d - 1, zpeer(d)) for d in ZFAR]
 
     def swap(v):
         return jnp.concatenate(
@@ -244,6 +245,9 @@
             ).astype(BF16)
         return [send(ipy.at[y], ipy.at[y], ip, 6 + d, ypeer(d)) for d in range(1, 4)]
 
+    for j in (1, 3, 2):
+        arrive([near[0, j], near[1, j]])
+        spread(j)
     load_table.wait()
     arrive(id2)
     idvec = sum_zc(idbuf[4:20])
@@ -266,11 +270,7 @@
         tcross.append(send(tsib_out.at[k], tsib_in.at[k], (txs, txr), k, sibling))
         tacc[k] = part[0:128].reshape(2, NX, 16, QUARTER)
 
-    target_rows(0)
-    for j in (1, 3, 2):
-        arrive([near[0, j], near[1, j]])
-        spread(j)
-    for k in range(1, 4):
+    for k in range(3):
         target_rows(k)
 
     cross = []
@@ -282,19 +282,20 @@
         cross.append(send(hall.at[0, 1, by], hall.at[1, 1, by], (css, csr), 2 * j + 1, sibling))
 
     group(0)
-    ipyc = sum_ipz()
+    group(1)
+    target_rows(3)
+    group(3)
+    group(2)
+
     for k in range(4):
         arrive([tcross[k]])
         tacc[k] = tacc[k] + tsib_in[k]
-    group(1)
-    group(3)
-    group(2)
-
     tfirst = []
     for k in range(3):
         tfirst.append(send(tacc.at[k, 0], tin0.at[k], (ts, tr), k, ypeer(FAR[k])))
         xx = (x + FAR[k]) % NX
         tfirst.append(send(tacc.at[:, 1, xx], tin1.at[k], (ts, tr), 3 + k, xpeer(FAR[k])))
+    ipyc = sum_ipz()
     arrive(cross)
 
     def tokens_of(yy):
@@ -445,7 +446,7 @@
         out3[zl, :, 0:PIECE] = pack(block[:, 0:SECT]).astype(BF16)
         out3[zl + 4, :, 0:PIECE] = pack(block[:, SECT:QUARTER]).astype(BF16)
     third = [
-        send(out3.at[(z + d) % NZ], in3.at[z], (r3s, r3r), d - 1, zpeer(d)) for d in range(1, NZ)
+        send(out3.at[(z + d) % NZ], in3.at[z], (r3s, r3r), d - 1, zpeer(d)) for d in ZFAR
     ]
     in3[z] = out3[z]
 

time: 62.3 us -> 59.9 us (0.961); the launches traced: 61.3 us -> 59.7 us
  Pallas kernels: 60.5 us -> 58.9 us
    pallas_call x1, Pallas kernels: 58.2 us -> 56.6 us  [per_device(): pl.pallas_call(kernel, out_shape=shapes, in_specs=[hbm] * 6, out_specs=(s...]
where the time goes in v4:
time: 59.9 us; the launch traced here: 59.7 us
  Pallas kernels  58.9 us (98%)
  between operations  0.8 us (1%)
    pallas_call x1, Pallas kernels, per_device(): pl.pallas_call(kernel, out_shape=shapes, in_specs=[hbm] * 6, out_specs=(s...  56.6 us
    pallas_call x1, Pallas kernels, per_device(): pl.pallas_call(hand_over, out_shape=shapes, in_specs=[smem, vmem, vmem],...  2.28 us

profile of v4, /device:TPU:1, one launch (start us, length us, event | category | flops | bytes accessed | tf_op | source)
XLA Modules:
  0.0 59.7 jit_solution(5750079188420504083)
XLA Ops:
  0.6 56.6 %shard_map.85 = (f32[8]{0:T(128)}, bf16[8,576]{1,0:T(8,128)(2,1)}, f32[1000,256]{1,0:T(8,128)}) custom-call(bf16[8,576]{1,0:T(8,128)(2,1)} %hidden_hbm.1, bf16[1000,4608]{1,0:T(8,128)(2,1)} %table_hbm.1, s32[8]{0:T(128)} %ids_hbm.1, s32[8]{0:T(128)} %targets_hbm.1, bf16[8,576]{1,0:T(8,128)(2,1)} %input_hbm.1, bf16[4608,256]{1,0:T(8,128)(2,1)} %proj_hbm.1), custom_call_target="tpu_custom_call" | custom-call | flops 8000000000 | bytes 13000000 | tf_op jit(solution)/shard_map/pallas_call | solution.py:519
  57.2 2.3 %shard_map.86 = (f32[8]{0:T(128)}, bf16[8,576]{1,0:T(8,128)(2,1)}, f32[1000,256]{1,0:T(8,128)}) custom-call(f32[8]{0:T(128)} %get-tuple-element.6.loss_in, bf16[8,576]{1,0:T(8,128)(2,1)} %get-tuple-element.7.grad_in, f32[1000,256]{1,0:T(8,128)} %get-tuple-element.8.low_in), custom_call_target="tpu_custom_call" | custom-call | tf_op jit(solution)/shard_map/pallas_call | solution.py:569

commit v5 on v4

--- a/solution.py
+++ b/solution.py
@@ -482,13 +482,15 @@
     store_low = pltpu.make_async_copy(low_ref, low_hbm, load_sem.at[6])
     store_low.start()
 
+    for copy in started[: -len(third)]:
+        copy.wait_send()
     arrive(third)
     grad = in3[0].astype(F32)
     for k in range(1, NZ):
         grad = grad + in3[k].astype(F32)
     grad_ref[...] = unpack(grad).astype(BF16)
     store_low.wait()
-    for copy in started:
+    for copy in third:
         copy.wait_send()
 
 

time: 59.9 us -> 59.7 us (level)
  no operation moved by 1% of the time
where the time goes in v5:
time: 59.7 us; the launch traced here: 59.4 us
  Pallas kernels  58.6 us (98%)
  between operations  0.8 us (1%)
    pallas_call x1, Pallas kernels, per_device(): pl.pallas_call(kernel, out_shape=shapes, in_specs=[hbm] * 6, out_specs=(s...  56.3 us
    pallas_call x1, Pallas kernels, per_device(): pl.pallas_call(hand_over, out_shape=shapes, in_specs=[smem, vmem, vmem],...  2.28 us

profile of v5, /device:TPU:1, one launch (start us, length us, event | category | flops | bytes accessed | tf_op | source)
XLA Modules:
  0.0 59.4 jit_solution(17373937588670634049)
XLA Ops:
  0.6 56.3 %shard_map.85 = (f32[8]{0:T(128)}, bf16[8,576]{1,0:T(8,128)(2,1)}, f32[1000,256]{1,0:T(8,128)}) custom-call(bf16[8,576]{1,0:T(8,128)(2,1)} %hidden_hbm.1, bf16[1000,4608]{1,0:T(8,128)(2,1)} %table_hbm.1, s32[8]{0:T(128)} %ids_hbm.1, s32[8]{0:T(128)} %targets_hbm.1, bf16[8,576]{1,0:T(8,128)(2,1)} %input_hbm.1, bf16[4608,256]{1,0:T(8,128)(2,1)} %proj_hbm.1), custom_call_target="tpu_custom_call" | custom-call | flops 8000000000 | bytes 13000000 | tf_op jit(solution)/shard_map/pallas_call | solution.py:521
  57.0 2.3 %shard_map.86 = (f32[8]{0:T(128)}, bf16[8,576]{1,0:T(8,128)(2,1)}, f32[1000,256]{1,0:T(8,128)}) custom-call(f32[8]{0:T(128)} %get-tuple-element.6.loss_in, bf16[8,576]{1,0:T(8,128)(2,1)} %get-tuple-element.7.grad_in, f32[1000,256]{1,0:T(8,128)} %get-tuple-element.8.low_in), custom_call_target="tpu_custom_call" | custom-call | tf_op jit(solution)/shard_map/pallas_call | solution.py:571
